TPU v7x, 128 devices: a whole 4x4x4 slice. The times are simulated.
128 devices in a mesh: gx: 2 (over core), gy: 64 (over z, y, x).
Axes of the slice: x: 4, y: 4, z: 4, core: 2. Of those that a mesh axis runs over, the one named last changes fastest.
Arguments:
- embeddings: bfloat16 [24576, 1024], P(('gx', 'gy'))
- cluster: int32 [24576], P(('gx', 'gy')), may hold values from 0 to 1, as said below
Outputs:
- best_similarity: float32 [24576], P(('gx', 'gy'))
Inputs may be any that keep to these rules, and one draw needn't show every extreme that they name: cluster modulo 2 is the owning index of gx; among the 192 documents of one device (aligned blocks) at most 144 have clusters with one owning index, and exactly 144 have one such owner in every block.
All inputs are finite; a program needn't handle non-finite values.
Results may differ from a plain program's by a relative error of at most 0.00048.
Values may be sent and summed in bfloat16 or wider, within the bound.
A program may use at most 128 MiB of HBM per device.

v0:
```python
import jax
import jax.numpy as jnp
from jax import lax
from jax.experimental import pallas as pl
from jax.experimental.pallas import tpu as pltpu
from jax.sharding import PartitionSpec as P

EPS = 1e-06
TURNS = (
    (0, 1, 2, 3, 4, 5),
    (0, 1, 2, 3, 5, 4),
    (0, 1, 3, 2, 4, 5),
    (0, 1, 3, 2, 5, 4),
    (1, 0, 2, 3, 4, 5),
    (1, 0, 2, 3, 5, 4),
    (1, 0, 3, 2, 4, 5),
    (1, 0, 3, 2, 5, 4),
)
TURN_OF = [0, 4, 4, 0, 2, 6, 6, 2, 2, 6, 6, 2, 0, 4, 4, 0, 1, 5, 5, 1, 3, 7, 7, 3, 3, 7, 7, 3, 1, 5, 5, 1, 1, 5, 5, 1, 3, 7, 7, 3, 3, 7, 7, 3, 1, 5, 5, 1, 0, 4, 4, 0, 2, 6, 6, 2, 2, 6, 6, 2, 0, 4, 4, 0]
SOURCES = (0, 4, 2, 1, 32, 20, 9, 3, 11, 48, 28, 60)
PARTS = ((0, 64), (64, 64), (128, 64))
TREES = (
    {1: (0, 3), 2: (0, 0), 3: (0, 1), 4: (0, 4), 5: (1, 5), 6: (3, 2), 7: (3, 1), 8: (7, 2), 9: (4, 4), 10: (5, 3), 11: (10, 5)},
    {1: (0, 3), 2: (0, 0), 3: (0, 1), 4: (0, 4), 5: (1, 5), 6: (3, 2), 7: (2, 0), 8: (6, 1), 9: (4, 4), 10: (5, 3), 11: (10, 5)},
    {1: (0, 3), 2: (0, 0), 3: (0, 1), 4: (0, 4), 5: (1, 5), 6: (3, 2), 7: (2, 0), 8: (6, 1), 9: (4, 4), 10: (5, 3), 11: (10, 5)},
)
CHILDREN = (
    {0: (1, 3, 4, 2), 1: (5,), 3: (7, 6), 4: (9,), 5: (10,), 7: (8,), 10: (11,)},
    {0: (1, 3, 2, 4), 1: (5,), 2: (7,), 3: (6,), 4: (9,), 5: (10,), 6: (8,), 10: (11,)},
    {0: (1, 3, 2, 4), 1: (5,), 2: (7,), 3: (6,), 4: (9,), 5: (10,), 6: (8,), 10: (11,)},
)
GROUP = 2
ROOT_ORDER = ((0, 1), (0, 3), (0, 4), (1, 2), (1, 1), (1, 3), (1, 4), (2, 2), (0, 2), (2, 1), (2, 3), (2, 4))
PAIRED = frozenset((0, 1, 2, 4, 5, 6, 7, 9))
SEGMENTS = (
    (
        (('d', 0), ('s',), ('f', 1, 0), ('f', 2, 1), ('f', 3, 0), ('f', 4, 0), ('f', 1, 1), ('f', 2, 2), ('f', 3, 1), ('f', 4, 1), ('f', 5, 0), ('f', 6, 0), ('f', 1, 2), ('f', 2, 0), ('f', 3, 2), ('f', 4, 2)),
        ((1, 0, 0),),
        (),
    ),
    (
        (('f', 5, 1), ('f', 6, 1), ('d', 1)),
        ((2, 0, 1),),
        (),
    ),
    (
        (('d', 2),),
        ((3, 1, 2), (4, 0, 1)),
        (),
    ),
    (
        (('f', 7, 0), ('f', 7, 1), ('f', 9, 0), ('f', 10, 0)),
        ((4, 2, 2),),
        (),
    ),
    (
        (('f', 5, 2), ('f', 6, 2), ('d', 4)),
        ((5, 2, 4), (6, 1, 2)),
        (),
    ),
    (
        (('f', 7, 2), ('f', 8, 1), ('f', 9, 1), ('f', 10, 1), ('d', 5)),
        ((3, 4, 5),),
        (),
    ),
    (
        (('f', 8, 0), ('f', 11, 0)),
        ((6, 5, 4), (7, 4, 5)),
        (),
    ),
    (
        (('f', 8, 2), ('f', 9, 2), ('f', 10, 2)),
        ((8, 1, 4), (9, 0, 5)),
        (),
    ),
    (
        (('f', 11, 1), ('d', 9)),
        ((8, 5, 9),),
        (),
    ),
    (
        (('d', 7),),
        ((9, 7, 2), (10, 0, 4)),
        (),
    ),
    (
        (('d', 6),),
        ((10, 2, 6),),
        (),
    ),
    (
        (('f', 11, 2),),
        ((11, 2, 7), (11, 9, 6), (9, 6, 6)),
        (1, 2, 3, 4, 5, 6, 7, 8, 0, 9, 10, 11),
    ),
)

MESH = pl.DeviceIdType.MESH
NSLOT = len(SOURCES)
NPART = len(PARTS)
NSEG = len(SEGMENTS)
LEFTS = [group[0] for _, groups, _ in SEGMENTS for group in groups]
RIGHTS = [[group[1 + u] for _, groups, _ in SEGMENTS for group in groups] for u in range(GROUP)]
BACKS = [slot for _, _, slots in SEGMENTS for slot in slots]
BACK_GROUP = 4
PAD = 256


def packed(digits, index):
    word = jnp.int32(0)
    for k in range(0, len(digits), 8):
        value = sum(d << (4 * j) for j, d in enumerate(digits[k : k + 8]))
        value = value - (1 << 32) if value >> 31 else value
        word = jnp.where(index // 8 == k // 8, jnp.int32(value), word)
    return lax.shift_right_logical(word, 4 * (index % 8)) & 15


def start_of(seg, column):
    first = jnp.int32(0)
    for k, segment in enumerate(SEGMENTS):
        if segment[column]:
            first = first + jnp.where(seg > k, len(segment[column]), 0)
    return first


def gray(code):
    return code ^ ((code >> 1) & 21)


def turned(turn, word):
    return sum(1 << TURNS[turn][k] for k in range(6) if word >> k & 1)


def kernel(
    x_hbm, c_hbm, o_ref, x_ref, c_ref, own, other, ids, side, best, back, back_out,
    load_sem, row_send, row_recv, pair_send, pair_recv, id_send, id_recv, back_send, back_recv,
):
    core = lax.axis_index("gx")
    place = lax.axis_index("gy")
    half = x_ref.shape[0]

    loads = [
        pltpu.make_async_copy(
            x_hbm.at[pl.ds(begin, size)], x_ref.at[pl.ds(begin, size)], load_sem.at[part]
        )
        for part, (begin, size) in enumerate(PARTS)
    ]
    loads.append(pltpu.make_async_copy(c_hbm, c_ref, load_sem.at[NPART]))
    for load in loads:
        load.start()

    corner = gray(place)
    turn = packed(TURN_OF, corner)

    def chip(word):
        values = [turned(t, word) for t in range(len(TURNS))]
        there = jnp.int32(values[0])
        for value in sorted(set(values) - {values[0]}):
            hits = turn < 0
            for t, v in enumerate(values):
                if v == value:
                    hits = hits | (turn == t)
            there = jnp.where(hits, value, there)
        return gray(corner ^ there)

    step_to = [chip(1 << k) for k in range(6)]

    barrier = pltpu.get_barrier_semaphore()
    for where in step_to:
        pl.semaphore_signal(barrier, inc=1, device_id=(core, where), device_id_type=MESH)
    pl.semaphore_signal(barrier, inc=1, device_id=(1 - core, place), device_id_type=MESH)

    source = [place] + [chip(w) for w in SOURCES[1:]]

    loads[NPART].wait()
    cluster = c_ref[...].astype(jnp.float32)
    ids[0, 0] = jnp.concatenate([cluster, jnp.full((1, PAD - half), -2.0, jnp.float32)], axis=1)

    def normalize(part):
        begin, size = PARTS[part]
        loads[part].wait()
        values = x_ref[begin : begin + size, :].astype(jnp.float32)
        total = jnp.sum(values * values, axis=1, keepdims=True)
        own[0, begin : begin + size, :] = (values * lax.rsqrt(total + EPS)).astype(jnp.bfloat16)

    def id_copy(slot):
        parent, step = TREES[0][slot]
        return pltpu.make_async_remote_copy(
            src_ref=ids.at[0, parent],
            dst_ref=ids.at[0, slot],
            send_sem=id_send.at[0, slot],
            recv_sem=id_recv.at[0, slot],
            device_id=(core, step_to[step]),
            device_id_type=MESH,
        )

    def id_pair_copy(slot):
        return pltpu.make_async_remote_copy(
            src_ref=ids.at[0, slot],
            dst_ref=ids.at[1, slot],
            send_sem=id_send.at[1, slot],
            recv_sem=id_recv.at[1, slot],
            device_id=(1 - core, place),
            device_id_type=MESH,
        )

    def back_copy(slot, which, where):
        return pltpu.make_async_remote_copy(
            src_ref=back_out.at[slot, which],
            dst_ref=back.at[slot, which],
            send_sem=back_send.at[slot, which],
            recv_sem=back_recv.at[slot, which],
            device_id=(1 - core if which else core, where),
            device_id_type=MESH,
        )

    def row_copy(part, slot):
        begin, size = PARTS[part]
        parent, step = TREES[part][slot]
        return pltpu.make_async_remote_copy(
            src_ref=own.at[parent, pl.ds(begin, size)],
            dst_ref=own.at[slot, pl.ds(begin, size)],
            send_sem=row_send.at[slot, part],
            recv_sem=row_recv.at[slot, part],
            device_id=(core, step_to[step]),
            device_id_type=MESH,
        )

    def pair_copy(slot, part):
        begin, size = PARTS[part]
        return pltpu.make_async_remote_copy(
            src_ref=own.at[slot, pl.ds(begin, size)],
            dst_ref=other.at[slot, pl.ds(begin, size)],
            send_sem=pair_send.at[slot, part],
            recv_sem=pair_recv.at[slot, part],
            device_id=(1 - core, place),
            device_id_type=MESH,
        )

    normalized = 0
    for part, slot in ROOT_ORDER:
        while normalized <= part:
            normalize(normalized)
            if normalized == 0:
                pl.semaphore_wait(barrier, 7)
            normalized += 1
        row_copy(part, slot).start()
        if part == 0:
            id_copy(slot).start()
    for part in range(normalized, NPART):
        normalize(part)
    id_pair_copy(0).start()
    for part in range(NPART):
        pair_copy(0, part).start()

    best[...] = jnp.full(best.shape, -1.0, jnp.float32)
    side[...] = jnp.full(side.shape, -1.0, jnp.float32)

    def forward(slot, part):
        row_copy(part, slot).wait_recv()
        for child in CHILDREN[part].get(slot, ()):
            row_copy(part, child).start()
        if slot in PAIRED:
            pair_copy(slot, part).start()
        if part == 0:
            id_copy(slot).wait_recv()
            for child in CHILDREN[part].get(slot, ()):
                id_copy(child).start()
            if slot in PAIRED:
                id_pair_copy(slot).start()

    def leave(part, slot):
        row_copy(part, slot).start()
        if part == 0:
            id_copy(slot).start()

    def take_pair(slot):
        id_pair_copy(slot).wait_recv()
        for part in range(NPART):
            pair_copy(slot, part).wait_recv()

    def give_back(index, carry):
        slots = [packed(BACKS, BACK_GROUP * index + u) for u in range(BACK_GROUP)]
        for slot in slots:
            padded = jnp.concatenate([side[slot], jnp.full((PAD - half, 128), -1.0, jnp.float32)], axis=0)
            turned_side = jnp.max(padded.T.reshape(128 // 8, 8, PAD), axis=0)
            turned_side = jnp.max(turned_side, axis=0, keepdims=True)
            high = jnp.max(best[slot], axis=0, keepdims=True)
            back_out[slot, 0, :, :half] = jnp.maximum(high[:, :half], turned_side[:, :half])
            back_out[slot, 1, :, :half] = high[:, half:]
        for slot in slots:
            where = source[0]
            whole = slot == 0
            for k in range(1, NSLOT):
                where = jnp.where(slot == k, source[k], where)
                if k in PAIRED:
                    whole = whole | (slot == k)

            @pl.when(slot > 0)
            def _():
                back_copy(slot, 0, where).start()

            @pl.when(whole)
            def _():
                back_copy(slot, 1, where).start()

        return carry

    def products_of(p, qs, same):
        right = jnp.concatenate([part for q in qs for part in (own[q], other[q])], axis=0)
        left_id = jnp.broadcast_to(ids[0, p], (128, PAD)).T[:half]
        right_ids = [jnp.concatenate([ids[0, q, :, :half], ids[1, q, :, :half]], axis=1) for q in qs]
        row_best = side[p]
        for begin in range(0, 2 * half * len(qs), PAD):
            end = min(begin + PAD, 2 * half * len(qs))
            products = lax.dot_general(
                own[p], right[begin:end], (((1,), (1,)), ((), ())), preferred_element_type=jnp.float32
            )
            for k in range(begin, end, 128):
                u, first = k // (2 * half), k % (2 * half)
                q, lanes = qs[u], slice(first, first + 128)
                allowed = left_id == right_ids[u][:, lanes]
                if same:
                    row = lax.broadcasted_iota(jnp.int32, (half, 128), 0)
                    column = lax.broadcasted_iota(jnp.int32, (half, 128), 1) + first
                    allowed = allowed & (row != column)
                masked = jnp.where(allowed, products[:, k - begin : k - begin + 128], -1.0)
                row_best = jnp.maximum(row_best, masked)
                best[q, :, lanes] = jnp.maximum(
                    best[q, :, lanes], jnp.max(masked.reshape(half // 8, 8, 128), axis=0)
                )
        side[p] = row_best

    def multiply(index, carry):
        products_of(packed(LEFTS, index), [packed(rights, index) for rights in RIGHTS], False)
        return carry

    actions = {
        "r": leave,
        "f": forward,
        "d": take_pair,
        "s": lambda: products_of(0, [0], True),
    }

    def segment(seg, carry):
        for k, (events, _, _) in enumerate(SEGMENTS):
            if events:

                @pl.when(seg == k)
                def _():
                    for name, *where in events:
                        actions[name](*where)

        lax.fori_loop(start_of(seg, 1), start_of(seg + 1, 1), multiply, carry)
        first, end = start_of(seg, 2) // BACK_GROUP, start_of(seg + 1, 2) // BACK_GROUP
        return lax.fori_loop(first, end, give_back, carry)

    lax.fori_loop(0, NSEG, segment, 0)

    for part in range(NPART):
        for slot in range(1, NSLOT):
            row_copy(part, slot).wait_send()
        for slot in sorted(PAIRED):
            pair_copy(slot, part).wait_send()
    for slot in sorted(PAIRED):
        id_pair_copy(slot).wait_send()
    for slot in range(1, NSLOT):
        id_copy(slot).wait_send()

    returned = [(slot, 0) for slot in range(1, NSLOT)] + [(slot, 1) for slot in sorted(PAIRED)]
    result = back_out[0, 0]
    for slot, which in returned:
        back_copy(slot, which, source[slot]).wait_recv()
        result = jnp.maximum(result, back[slot, which])
    o_ref[...] = result[:, :half]

    for slot, which in returned:
        back_copy(slot, which, source[slot]).wait_send()


def local(embeddings, cluster):
    half, width = embeddings.shape
    best = pl.pallas_call(
        kernel,
        out_shape=jax.ShapeDtypeStruct((1, half), jnp.float32),
        in_specs=[pl.BlockSpec(memory_space=pl.ANY)] * 2,
        out_specs=pl.BlockSpec(memory_space=pltpu.VMEM),
        scratch_shapes=[
            pltpu.VMEM((half, width), jnp.bfloat16),
            pltpu.VMEM((1, half), jnp.int32),
            pltpu.VMEM((NSLOT, half, width), jnp.bfloat16),
            pltpu.VMEM((NSLOT, half, width), jnp.bfloat16),
            pltpu.VMEM((2, NSLOT, 1, PAD), jnp.float32),
            pltpu.VMEM((NSLOT, half, 128), jnp.float32),
            pltpu.VMEM((NSLOT, 8, 2 * half), jnp.float32),
            pltpu.VMEM((NSLOT, 2, 1, PAD), jnp.float32),
            pltpu.VMEM((NSLOT, 2, 1, PAD), jnp.float32),
            pltpu.SemaphoreType.DMA((NPART + 1,)),
            pltpu.SemaphoreType.DMA((NSLOT, NPART)),
            pltpu.SemaphoreType.DMA((NSLOT, NPART)),
            pltpu.SemaphoreType.DMA((NSLOT, NPART)),
            pltpu.SemaphoreType.DMA((NSLOT, NPART)),
            pltpu.SemaphoreType.DMA((2, NSLOT)),
            pltpu.SemaphoreType.DMA((2, NSLOT)),
            pltpu.SemaphoreType.DMA((NSLOT, 2)),
            pltpu.SemaphoreType.DMA((NSLOT, 2)),
        ],
        compiler_params=pltpu.CompilerParams(
            collective_id=0, has_side_effects=True, vmem_limit_bytes=56 * 1024 * 1024
        ),
        cost_estimate=pl.CostEstimate(
            flops=4 * GROUP * len(LEFTS) * half * half * width, bytes_accessed=2 * half * width, transcendentals=half
        ),
    )(embeddings, cluster.reshape(1, half))
    return jnp.maximum(best.reshape(half), -1.0)


def solution(mesh):
    return jax.shard_map(
        local,
        mesh=mesh,
        in_specs=(P(("gx", "gy"), None), P(("gx", "gy"))),
        out_specs=P(("gx", "gy")),
        check_vma=False,
    )
```

profile of v0, /device:TPU:1, one launch (start us, length us, event | category | flops | bytes accessed | tf_op | source)
XLA Modules:
  0.0 47.1 jit_solution(435410666945487692)
XLA Ops:
  0.0 45.8 %shard_map.28 = f32[1,192]{1,0:T(1,128)} custom-call(bf16[192,1024]{1,0:T(8,128)(2,1)} %x_hbm.1, s32[1,192]{1,0:T(1,128)} %bitcast.2), custom_call_target="tpu_custom_call" | custom-call | flops 5737807872 | bytes 393216 | tf_op jit(solution)/shard_map/pallas_call | solution.py:383
  45.8 1.2 %broadcast_maximum_fusion = f32[1,192]{1,0:T(1,128)} fusion(f32[1,192]{1,0:T(1,128)} %shard_map.28), kind=kLoop, calls=%fused_computation | loop fusion | flops 192 | bytes 1536 | tf_op jit(solution)/shard_map/max | solution.py:415
where the time goes:
time: 47.2 us; the launch traced here: 47.1 us
  Pallas kernels  45.8 us (97%)
  other arithmetic  1.24 us (3%)
    pallas_call x1, Pallas kernels, local(): pl.pallas_call(kernel, out_shape=jax.ShapeDtypeStruct((1, half), jnp.floa...  45.8 us
    max x1, other arithmetic, local(): return jnp.maximum(best.reshape(half), -1.0)  1.24 us

commit v1 on v0

--- a/solution.py
+++ b/solution.py
@@ -31,7 +31,7 @@
 )
 GROUP = 2
 ROOT_ORDER = ((0, 1), (0, 3), (0, 4), (1, 2), (1, 1), (1, 3), (1, 4), (2, 2), (0, 2), (2, 1), (2, 3), (2, 4))
-PAIRED = frozenset((0, 1, 2, 4, 5, 6, 7, 9))
+PAIRED = frozenset((0, 1, 2, 3, 4, 5, 6, 7, 9))
 SEGMENTS = (
     (
         (('d', 0), ('s',), ('f', 1, 0), ('f', 2, 1), ('f', 3, 0), ('f', 4, 0), ('f', 1, 1), ('f', 2, 2), ('f', 3, 1), ('f', 4, 1), ('f', 5, 0), ('f', 6, 0), ('f', 1, 2), ('f', 2, 0), ('f', 3, 2), ('f', 4, 2)),
@@ -45,31 +45,31 @@
     ),
     (
         (('d', 2),),
-        ((3, 1, 2), (4, 0, 1)),
+        ((3, 1, 2),),
+        (),
+    ),
+    (
+        (('d', 3),),
+        ((4, 3, 0),),
         (),
     ),
     (
         (('f', 7, 0), ('f', 7, 1), ('f', 9, 0), ('f', 10, 0)),
-        ((4, 2, 2),),
+        ((4, 1, 2),),
         (),
     ),
     (
         (('f', 5, 2), ('f', 6, 2), ('d', 4)),
-        ((5, 2, 4), (6, 1, 2)),
+        ((5, 3, 4), (6, 1, 4), (5, 2, 2)),
         (),
     ),
     (
         (('f', 7, 2), ('f', 8, 1), ('f', 9, 1), ('f', 10, 1), ('d', 5)),
-        ((3, 4, 5),),
-        (),
-    ),
-    (
-        (('f', 8, 0), ('f', 11, 0)),
-        ((6, 5, 4), (7, 4, 5)),
-        (),
-    ),
-    (
-        (('f', 8, 2), ('f', 9, 2), ('f', 10, 2)),
+        ((6, 2, 5), (7, 4, 5)),
+        (),
+    ),
+    (
+        (('f', 8, 0), ('f', 11, 0), ('f', 8, 2), ('f', 9, 2), ('f', 10, 2)),
         ((8, 1, 4), (9, 0, 5)),
         (),
     ),
@@ -85,13 +85,13 @@
     ),
     (
         (('d', 6),),
-        ((10, 2, 6),),
-        (),
+        ((10, 2, 6), (9, 6, 6)),
+        (8, 10, 5, 1),
     ),
     (
         (('f', 11, 2),),
-        ((11, 2, 7), (11, 9, 6), (9, 6, 6)),
-        (1, 2, 3, 4, 5, 6, 7, 8, 0, 9, 10, 11),
+        ((11, 2, 6), (11, 7, 9)),
+        (11, 6, 7, 9, 2, 3, 4, 0),
     ),
 )
 

time: 47.2 us -> 46.6 us (0.987)
  Pallas kernels: 45.8 us -> 45.1 us
    pallas_call x1, Pallas kernels: 45.8 us -> 45.1 us  [local(): pl.pallas_call(kernel, out_shape=jax.ShapeDtypeStruct((1, half), jnp.floa...]
where the time goes in v1:
time: 46.6 us; the launch traced here: 46.4 us
  Pallas kernels  45.1 us (97%)
  other arithmetic  1.24 us (3%)
    pallas_call x1, Pallas kernels, local(): pl.pallas_call(kernel, out_shape=jax.ShapeDtypeStruct((1, half), jnp.floa...  45.1 us
    max x1, other arithmetic, local(): return jnp.maximum(best.reshape(half), -1.0)  1.24 us

profile of v1, /device:TPU:1, one launch (start us, length us, event | category | flops | bytes accessed | tf_op | source)
XLA Modules:
  0.0 46.4 jit_solution(1644887934799093205)
XLA Ops:
  0.0 45.1 %shard_map.28 = f32[1,192]{1,0:T(1,128)} custom-call(bf16[192,1024]{1,0:T(8,128)(2,1)} %x_hbm.1, s32[1,192]{1,0:T(1,128)} %bitcast.2), custom_call_target="tpu_custom_call" | custom-call | flops 5737807872 | bytes 393216 | tf_op jit(solution)/shard_map/pallas_call | solution.py:383
  45.1 1.2 %broadcast_maximum_fusion = f32[1,192]{1,0:T(1,128)} fusion(f32[1,192]{1,0:T(1,128)} %shard_map.28), kind=kLoop, calls=%fused_computation | loop fusion | flops 192 | bytes 1536 | tf_op jit(solution)/shard_map/max | solution.py:415

commit v2 on v1

--- a/solution.py
+++ b/solution.py
@@ -102,7 +102,7 @@
 LEFTS = [group[0] for _, groups, _ in SEGMENTS for group in groups]
 RIGHTS = [[group[1 + u] for _, groups, _ in SEGMENTS for group in groups] for u in range(GROUP)]
 BACKS = [slot for _, _, slots in SEGMENTS for slot in slots]
-BACK_GROUP = 4
+BACK_GROUP = 2
 PAD = 256
 
 

time: 46.6 us -> 46.7 us (level)
  no operation moved by 1% of the time
where the time goes in v2:
time: 46.7 us; the launch traced here: 46.5 us
  Pallas kernels  45.3 us (97%)
  other arithmetic  1.24 us (3%)
    pallas_call x1, Pallas kernels, local(): pl.pallas_call(kernel, out_shape=jax.ShapeDtypeStruct((1, half), jnp.floa...  45.3 us
    max x1, other arithmetic, local(): return jnp.maximum(best.reshape(half), -1.0)  1.24 us

profile of v2, /device:TPU:1, one launch (start us, length us, event | category | flops | bytes accessed | tf_op | source)
XLA Modules:
  0.0 46.5 jit_solution(14531801375946522256)
XLA Ops:
  0.0 45.3 %shard_map.28 = f32[1,192]{1,0:T(1,128)} custom-call(bf16[192,1024]{1,0:T(8,128)(2,1)} %x_hbm.1, s32[1,192]{1,0:T(1,128)} %bitcast.2), custom_call_target="tpu_custom_call" | custom-call | flops 5737807872 | bytes 393216 | tf_op jit(solution)/shard_map/pallas_call | solution.py:383
  45.3 1.2 %broadcast_maximum_fusion = f32[1,192]{1,0:T(1,128)} fusion(f32[1,192]{1,0:T(1,128)} %shard_map.28), kind=kLoop, calls=%fused_computation | loop fusion | flops 192 | bytes 1536 | tf_op jit(solution)/shard_map/max | solution.py:415

commit v3 on v2

--- a/solution.py
+++ b/solution.py
@@ -102,7 +102,7 @@
 LEFTS = [group[0] for _, groups, _ in SEGMENTS for group in groups]
 RIGHTS = [[group[1 + u] for _, groups, _ in SEGMENTS for group in groups] for u in range(GROUP)]
 BACKS = [slot for _, _, slots in SEGMENTS for slot in slots]
-BACK_GROUP = 2
+BACK_GROUP = 1
 PAD = 256
 
 

time: 46.7 us -> 46.9 us (level)
  no operation moved by 1% of the time
where the time goes in v3:
time: 46.9 us; the launch traced here: 46.8 us
  Pallas kernels  45.5 us (97%)
  other arithmetic  1.24 us (3%)
    pallas_call x1, Pallas kernels, local(): pl.pallas_call(kernel, out_shape=jax.ShapeDtypeStruct((1, half), jnp.floa...  45.5 us
    max x1, other arithmetic, local(): return jnp.maximum(best.reshape(half), -1.0)  1.24 us

profile of v3, /device:TPU:1, one launch (start us, length us, event | category | flops | bytes accessed | tf_op | source)
XLA Modules:
  0.0 46.8 jit_solution(11194796475313702921)
XLA Ops:
  0.0 45.5 %shard_map.28 = f32[1,192]{1,0:T(1,128)} custom-call(bf16[192,1024]{1,0:T(8,128)(2,1)} %x_hbm.1, s32[1,192]{1,0:T(1,128)} %bitcast.2), custom_call_target="tpu_custom_call" | custom-call | flops 5737807872 | bytes 393216 | tf_op jit(solution)/shard_map/pallas_call | solution.py:383
  45.5 1.2 %broadcast_maximum_fusion = f32[1,192]{1,0:T(1,128)} fusion(f32[1,192]{1,0:T(1,128)} %shard_map.28), kind=kLoop, calls=%fused_computation | loop fusion | flops 192 | bytes 1536 | tf_op jit(solution)/shard_map/max | solution.py:415
